TPU v7x, 128 devices: a whole 4x4x4 slice. The times are simulated.
128 devices in a mesh: dp: 8 (over z, core), fsdp: 16 (over y, x).
Axes of the slice: x: 4, y: 4, z: 4, core: 2. Of those that a mesh axis runs over, the one named last changes fastest.
Arguments:
- partials: bfloat16 [8, 64, 1024, 1024], P('dp', None, 'fsdp'), may hold values from -5 to 5
- first_moment: float32 [64, 1024, 1024], P('dp', 'fsdp'), may hold values from -6 to 6
- second_moment: float32 [64, 1024, 1024], P('dp', 'fsdp'), may hold values from 0.05 to 5
- step_counts: int32 [64], replicated, may hold values from 1 to 199
- owners: int32 [64], replicated, may hold values from 0 to 15, as said below
- left_basis: bfloat16 [8, 16, 1024, 1024], P('dp', 'fsdp'), may hold values from -0.1875 to 0.1875
- right_basis: bfloat16 [8, 16, 1024, 1024], P('dp', 'fsdp'), may hold values from -0.1875 to 0.1875
Outputs:
- update: bfloat16 [64, 1024, 1024], P('dp', 'fsdp')
- new_first: float32 [64, 1024, 1024], P('dp', 'fsdp')
- new_second: float32 [64, 1024, 1024], P('dp', 'fsdp')
Inputs may be any that keep to these rules, and one draw needn't show every extreme that they name: Within each aligned group of 8 blocks (blocks g * 8 to g * 8 + 7) the owners are distinct fsdp indices.
All inputs are finite; a program needn't handle non-finite values.
Results may differ from a plain program's by a relative error of at most 0.017.
Values may be sent and summed in bfloat16 or wider, within the bound.
A program may use at most 192 MiB of HBM per device.

v0:
```python
import jax
import jax.numpy as jnp
from jax import lax
from jax.sharding import PartitionSpec as P

BETA_ONE = 0.9
BETA_TWO = 0.95
EPSILON = 1e-08


def adam_step(rotated, first_moment, second_moment, step_count):
    moment_one = BETA_ONE * first_moment + (1.0 - BETA_ONE) * rotated
    moment_two = BETA_TWO * second_moment + (1.0 - BETA_TWO) * rotated * rotated
    correct_one = 1.0 - jnp.power(BETA_ONE, step_count)
    correct_two = 1.0 - jnp.power(BETA_TWO, step_count)
    direction = (moment_one / correct_one / (jnp.sqrt(moment_two / correct_two) + EPSILON)).astype(
        jnp.bfloat16
    )
    return (direction, moment_one, moment_two)


def turn_forward(left_matrix, gradient, right_matrix):
    half_turn = lax.dot_general(
        left_matrix, gradient, (((0,), (0,)), ((), ())), preferred_element_type=jnp.float32
    ).astype(jnp.bfloat16)
    return jnp.dot(half_turn, right_matrix, preferred_element_type=jnp.float32)


def turn_back(left_matrix, direction, right_matrix):
    half_turn = jnp.dot(left_matrix, direction, preferred_element_type=jnp.float32).astype(
        jnp.bfloat16
    )
    return lax.dot_general(
        half_turn, right_matrix, (((1,), (1,)), ((), ())), preferred_element_type=jnp.float32
    ).astype(jnp.bfloat16)


def shards(partials, first_moment, second_moment, step_counts, owners, left_basis, right_basis):
    group_index = lax.axis_index("dp")
    member_index = lax.axis_index("fsdp")
    members = lax.axis_size("fsdp")
    local_blocks = first_moment.shape[0]
    strip_rows = first_moment.shape[1]
    columns = first_moment.shape[2]
    left_matrix = left_basis[0, 0]
    right_matrix = right_basis[0, 0]
    group_owners = lax.dynamic_slice_in_dim(owners, group_index * local_blocks, local_blocks)
    group_counts = lax.dynamic_slice_in_dim(step_counts, group_index * local_blocks, local_blocks)
    member_ids = jnp.arange(members, dtype=jnp.int32)
    matches = group_owners[None, :] == member_ids[:, None]
    has_block = jnp.any(matches, axis=1)
    slot_of = jnp.sum(
        jnp.where(matches, jnp.arange(local_blocks, dtype=jnp.int32)[None, :], 0), axis=1
    )
    own_count = jnp.maximum(
        jnp.sum(jnp.where(group_owners == member_index, group_counts, 0)), 1
    ).astype(jnp.float32)

    def pack_slots(strips):
        picked = jnp.take(strips, slot_of, axis=0)
        return jnp.where(has_block[:, None, None], picked, jnp.zeros_like(picked))

    def unpack(received):
        return jnp.take(received, group_owners, axis=0)

    def as_block(received):
        return received.reshape(members * strip_rows, columns)

    def as_strips(block_rows):
        return block_rows.reshape(members, strip_rows, columns)

    group_sums = lax.psum_scatter(
        partials[0].astype(jnp.float32).astype(jnp.bfloat16), "dp", scatter_dimension=0, tiled=True
    ).astype(jnp.float32)
    strips_in, own_first, own_second = (
        lax.all_to_all(pack_slots(group_sums), "fsdp", split_axis=0, concat_axis=0, tiled=True),
        lax.all_to_all(pack_slots(first_moment), "fsdp", split_axis=0, concat_axis=0, tiled=True),
        lax.all_to_all(pack_slots(second_moment), "fsdp", split_axis=0, concat_axis=0, tiled=True),
    )
    gradient = as_block(strips_in)
    rotated = turn_forward(left_matrix, gradient.astype(jnp.bfloat16), right_matrix)
    direction, moment_one, moment_two = adam_step(
        rotated, as_block(own_first), as_block(own_second), own_count
    )
    first_home, second_home = (
        lax.all_to_all(
            as_strips(moment_one).astype(jnp.bfloat16),
            "fsdp",
            split_axis=0,
            concat_axis=0,
            tiled=True,
        ).astype(jnp.float32),
        lax.all_to_all(
            as_strips(moment_two).astype(jnp.bfloat16),
            "fsdp",
            split_axis=0,
            concat_axis=0,
            tiled=True,
        ).astype(jnp.float32),
    )
    first_out = unpack(first_home)
    second_out = unpack(second_home)
    update_block = turn_back(left_matrix, direction, right_matrix)
    update_strips = unpack(
        lax.all_to_all(as_strips(update_block), "fsdp", split_axis=0, concat_axis=0, tiled=True)
    )
    return (update_strips, first_out, second_out)


def solution(mesh):
    placed = (
        P("dp", None, "fsdp", None),
        P("dp", "fsdp", None),
        P("dp", "fsdp", None),
        P(),
        P(),
        P("dp", "fsdp", None, None),
        P("dp", "fsdp", None, None),
    )
    return jax.shard_map(
        shards,
        mesh=mesh,
        in_specs=placed,
        out_specs=(P("dp", "fsdp", None), P("dp", "fsdp", None), P("dp", "fsdp", None)),
        check_vma=False,
    )
```

profile of v0, /device:TPU:0, one launch (start us, length us, event | category | flops | bytes accessed | tf_op | source)
XLA Modules:
  0.0 301.7 jit_solution(127181126926838590)
XLA Ops:
  7.2 0.0 copy-start
  7.2 0.0 reduce-scatter.2.cloned.1.call-start
  7.2 0.0 copy-start.1
  7.2 0.7 reduce-scatter.2.cloned.1.call-update
  7.9 0.1 copy-done.1
  8.0 0.1 compare_and_fusion.1
  8.1 0.1 select_reduce_fusion
  8.2 4.3 %gather_fusion.1 = f32[16,64,1024]{2,1,0:T(8,128)} fusion(f32[8,64,1024]{2,1,0:T(8,128)} %param.12, s32[1024]{0:T(1024)S(1)} %pad_clamp_fusion.1), kind=kCustom, calls=%fused_computation.clone | custom fusion | bytes 8388672 | tf_op jit(solution)/shard_map/jit(_take)/gather | solution.py:60
  12.5 4.4 %gather_fusion.3 = f32[16,64,1024]{2,1,0:T(8,128)} fusion(f32[8,64,1024]{2,1,0:T(8,128)} %param.13, s32[1024]{0:T(1024)S(1)} %pad_clamp_fusion.1), kind=kCustom, calls=%fused_computation.3.clone | custom fusion | bytes 8388672 | tf_op jit(solution)/shard_map/jit(_take)/gather | solution.py:60
  16.9 0.1 fusion.26
  17.0 7.0 %select_select_fusion = (f32[16,64,1024]{2,1,0:T(8,128)S(1)}, f32[16,64,1024]{2,1,0:T(8,128)}) fusion(f32[16,64,1024]{2,1,0:T(8,128)} %gather_fusion.3, pred[16]{0:T(512)(128)(4,1)S(1)} %compare_and_fusion, pred[16]{0:T(512)(128)(4,1)S(1)} %fusion.26, f32[16,64,1024]{2,1,0:T(8,128)} %gather_fusion.1), kind=kLoop, calls=%fused_computation.9 | loop fusion | flops 4194304 | bytes 16777248 | tf_op jit(solution)/shard_map/jit(_where)/select_n | solution.py:61
  24.1 57.9 %all_to_all.30 = f32[16,64,1024]{2,1,0:T(8,128)} all-to-all(f32[16,64,1024]{2,1,0:T(8,128)S(1)} %get-tuple-element.13), channel_id=1, replica_groups=mesh['dp'=8,'fsdp'=16] {'fsdp'}, dimensions={0} | all-to-all | bytes 8388608 | tf_op jit(solution)/shard_map/all_to_all | solution.py:78
  81.9 4.5 %all-to-all-start = ((f32[16,64,1024]{2,1,0:T(8,128)}), f32[16,64,1024]{2,1,0:T(8,128)}, u32[]{:S(2)}, u32[]{:S(2)}) async-start(f32[16,64,1024]{2,1,0:T(8,128)} %get-tuple-element.14), calls=%async_computation | async-start | bytes 8388608 | tf_op jit(solution)/shard_map/all_to_all | solution.py:77
  86.5 0.0 reduce-scatter.2.cloned.1.call-done
  86.5 3.2 %gather_fusion.2 = bf16[16,64,1024]{2,1,0:T(8,128)(2,1)} fusion(bf16[8,64,1024]{2,1,0:T(8,128)(2,1)} %reduce-scatter.2.cloned.1.call-done, s32[1024]{0:T(1024)S(1)} %pad_clamp_fusion.1), kind=kCustom, calls=%fused_computation.2.clone | custom fusion | bytes 4194368 | tf_op jit(solution)/shard_map/jit(_take)/gather | solution.py:60
  89.7 3.8 %select_select_fusion.1 = bf16[16,64,1024]{2,1,0:T(8,128)(2,1)} fusion(bf16[16,64,1024]{2,1,0:T(8,128)(2,1)} %gather_fusion.2, pred[16]{0:T(512)(128)(4,1)S(1)} %compare_and_fusion, pred[16]{0:T(512)(128)(4,1)S(1)} %fusion.26), kind=kLoop, calls=%fused_computation.10 | loop fusion | flops 2097152 | bytes 4194336 | tf_op jit(solution)/shard_map/jit(_where)/select_n | solution.py:61
  93.5 53.3 %all-to-all-done = f32[16,64,1024]{2,1,0:T(8,128)} async-done(((f32[16,64,1024]{2,1,0:T(8,128)}), f32[16,64,1024]{2,1,0:T(8,128)}, u32[]{:S(2)}, u32[]{:S(2)}) %all-to-all-start) | async-done | bytes 4194336 | tf_op jit(solution)/shard_map/all_to_all | solution.py:77
  146.8 4.4 %all-to-all-start.1 = ((bf16[16,64,1024]{2,1,0:T(8,128)(2,1)}), bf16[16,64,1024]{2,1,0:T(8,128)(2,1)}, u32[]{:S(2)}, u32[]{:S(2)}) async-start(bf16[16,64,1024]{2,1,0:T(8,128)(2,1)} %select_select_fusion.1), calls=%async_computation.2 | async-start | bytes 4194304 | tf_op jit(solution)/shard_map/all_to_all | solution.py:76
  151.2 5.0 %broadcast_multiply_fusion = f32[16,64,1024]{2,1,0:T(8,128)} fusion(f32[16,64,1024]{2,1,0:T(8,128)} %all_to_all.30), kind=kLoop, calls=%fused_computation.22 | loop fusion | flops 1048576 | bytes 8388608 | tf_op jit(solution)/shard_map/mul | solution.py:13
  156.3 5.1 %broadcast_multiply_fusion.1 = f32[16,64,1024]{2,1,0:T(8,128)} fusion(f32[16,64,1024]{2,1,0:T(8,128)} %all-to-all-done), kind=kLoop, calls=%fused_computation.24 | loop fusion | flops 1048576 | bytes 8388608 | tf_op jit(solution)/shard_map/mul | solution.py:12
  161.4 18.1 %all-to-all-done.1 = bf16[16,64,1024]{2,1,0:T(8,128)(2,1)} async-done(((bf16[16,64,1024]{2,1,0:T(8,128)(2,1)}), bf16[16,64,1024]{2,1,0:T(8,128)(2,1)}, u32[]{:S(2)}, u32[]{:S(2)}) %all-to-all-start.1) | async-done | bytes 2097184 | tf_op jit(solution)/shard_map/all_to_all | solution.py:76
  179.4 0.0 copy-done
  179.5 11.7 %fusion.21 = (bf16[1024,1024]{1,0:T(8,128)(2,1)}, f32[1024,1024]{1,0:T(8,128)}, f32[1024,1024]{1,0:T(8,128)}, bf16[1024,1024]{1,0:T(8,128)(2,1)}) fusion(f32[16,64,1024]{2,1,0:T(8,128)} %broadcast_multiply_fusion, f32[16,64,1024]{2,1,0:T(8,128)} %broadcast_multiply_fusion.1, bf16[1,1,1024,1024]{3,2,1,0:T(8,128)(2,1)S(1)} %copy-done, ...), kind=kOutput, calls=%fused_computation.27 | convolution fusion | flops 4303355904 | bytes 27262976 | tf_op jit(solution)/shard_map/dot_general | solution.py:26
  191.1 0.0 copy-start.2
  191.1 31.3 %all_to_all.31 = bf16[16,64,1024]{2,1,0:T(8,128)(2,1)} all-to-all(bf16[16,64,1024]{2,1,0:T(8,128)(2,1)} %bitcast.41), channel_id=1, replica_groups=mesh['dp'=8,'fsdp'=16] {'fsdp'}, dimensions={0} | all-to-all | bytes 4194304 | tf_op jit(solution)/shard_map/all_to_all | solution.py:93
  222.4 4.6 %all-to-all-start.4 = ((bf16[16,64,1024]{2,1,0:T(8,128)(2,1)}), bf16[16,64,1024]{2,1,0:T(8,128)(2,1)}, u32[]{:S(2)}, u32[]{:S(2)}) async-start(bf16[16,64,1024]{2,1,0:T(8,128)(2,1)} %bitcast.39), calls=%async_computation.5 | async-start | bytes 4194304 | tf_op jit(solution)/shard_map/all_to_all | solution.py:86
  227.0 0.0 copy-done.2
  227.1 0.7 compare_select_fusion.1
  228.5 11.2 %fusion.11 = bf16[1024,1024]{1,0:T(8,128)(2,1)} fusion(bf16[1,1,1024,1024]{3,2,1,0:T(8,128)(2,1)S(1)} %copy-done, bf16[1,1,1024,1024]{3,2,1,0:T(8,128)(2,1)} %param.16, f32[1024,1024]{1,0:T(8,128)} %get-tuple-element.11, f32[1024,1024]{1,0:T(8,128)} %get-tuple-element.8, f32[]{:T(128)S(6)} %sub.7, f32[]{:T(128)S(6)} %sub.6), kind=kOutput, calls=%fused_computation.25 | convolution fusion | flops 4302307328 | bytes 14680072 | tf_op jit(solution)/shard_map/dot_general | solution.py:33
  239.7 14.6 %all-to-all-done.4 = bf16[16,64,1024]{2,1,0:T(8,128)(2,1)} async-done(((bf16[16,64,1024]{2,1,0:T(8,128)(2,1)}), bf16[16,64,1024]{2,1,0:T(8,128)(2,1)}, u32[]{:S(2)}, u32[]{:S(2)}) %all-to-all-start.4) | async-done | bytes 2097184 | tf_op jit(solution)/shard_map/all_to_all | solution.py:86
  254.4 4.4 %all-to-all-start.3 = ((bf16[16,64,1024]{2,1,0:T(8,128)(2,1)}), bf16[16,64,1024]{2,1,0:T(8,128)(2,1)}, u32[]{:S(2)}, u32[]{:S(2)}) async-start(bf16[16,64,1024]{2,1,0:T(8,128)(2,1)} %bitcast.40), calls=%async_computation.4 | async-start | bytes 4194304 | tf_op jit(solution)/shard_map/all_to_all | solution.py:105
  258.8 4.0 %convert_element_type.59 = f32[16,64,1024]{2,1,0:T(8,128)} convert(bf16[16,64,1024]{2,1,0:T(8,128)(2,1)} %all_to_all.31) | non-fusion elementwise | flops 1048576 | bytes 6291456 | tf_op jit(solution)/shard_map/convert_element_type | solution.py:99
  262.8 4.2 %gather_fusion.5 = f32[8,64,1024]{2,1,0:T(8,128)} fusion(f32[16,64,1024]{2,1,0:T(8,128)} %convert_element_type.59, s32[1024]{0:T(1024)S(1)} %pad_clamp_fusion), kind=kCustom, calls=%fused_computation.4.clone | custom fusion | bytes 4194336 | tf_op jit(solution)/shard_map/jit(_take)/gather | solution.py:64
  267.0 4.0 %convert_element_type.56 = f32[16,64,1024]{2,1,0:T(8,128)} convert(bf16[16,64,1024]{2,1,0:T(8,128)(2,1)} %all-to-all-done.4) | non-fusion elementwise | flops 1048576 | bytes 6291456 | tf_op jit(solution)/shard_map/convert_element_type | solution.py:92
  271.0 4.2 %gather_fusion.4 = f32[8,64,1024]{2,1,0:T(8,128)} fusion(f32[16,64,1024]{2,1,0:T(8,128)} %convert_element_type.56, s32[1024]{0:T(1024)S(1)} %pad_clamp_fusion), kind=kCustom, calls=%fused_computation.1.clone | custom fusion | bytes 4194336 | tf_op jit(solution)/shard_map/jit(_take)/gather | solution.py:64
  275.2 11.2 %all-to-all-done.3 = bf16[16,64,1024]{2,1,0:T(8,128)(2,1)} async-done(((bf16[16,64,1024]{2,1,0:T(8,128)(2,1)}), bf16[16,64,1024]{2,1,0:T(8,128)(2,1)}, u32[]{:S(2)}, u32[]{:S(2)}) %all-to-all-start.3) | async-done | bytes 2097184 | tf_op jit(solution)/shard_map/all_to_all | solution.py:105
  286.4 2.2 gather_fusion
  288.6 1.1 broadcast_select_fusion.2
  289.7 5.1 %broadcast_select_fusion = (f32[8,64,1024]{2,1,0:T(8,128)}, f32[8,64,1024]{2,1,0:T(8,128)}) fusion(f32[8,64,1024]{2,1,0:T(8,128)} %gather_fusion.5, pred[8]{0:T(512)(128)(4,1)S(1)} %get-tuple-element.5, f32[8,64,1024]{2,1,0:T(8,128)} %gather_fusion.4), kind=kLoop, calls=%fused_computation.28 | loop fusion | flops 1048576 | bytes 8388616 | tf_op jit(solution)/shard_map/jit(_take)/select_n | solution.py:64
  (4 shorter events, 0.0 us)
Async XLA Ops:
  7.2 172.3 %copy-start = (bf16[1,1,1024,1024]{3,2,1,0:T(8,128)(2,1)S(1)}, bf16[1,1,1024,1024]{3,2,1,0:T(8,128)(2,1)}, u32[]{:S(2)}) copy-start(bf16[1,1,1024,1024]{3,2,1,0:T(8,128)(2,1)} %param.17) | copy-start | bytes 6291460
  7.2 79.3 %reduce-scatter.2.cloned.1.call-start = ((), (), s32[]{:S(2)}) async-start(), calls=%async_computation.7 | async-start | bytes 9437184 | tf_op jit(solution)/shard_map/reduce_scatter | solution.py:72
  7.2 0.8 copy-start.1
  81.9 64.9 %all-to-all-start = ((f32[16,64,1024]{2,1,0:T(8,128)}), f32[16,64,1024]{2,1,0:T(8,128)}, u32[]{:S(2)}, u32[]{:S(2)}) async-start(f32[16,64,1024]{2,1,0:T(8,128)} %get-tuple-element.14), calls=%async_computation | async-start | bytes 8388608 | tf_op jit(solution)/shard_map/all_to_all | solution.py:77
  146.8 32.7 %all-to-all-start.1 = ((bf16[16,64,1024]{2,1,0:T(8,128)(2,1)}), bf16[16,64,1024]{2,1,0:T(8,128)(2,1)}, u32[]{:S(2)}, u32[]{:S(2)}) async-start(bf16[16,64,1024]{2,1,0:T(8,128)(2,1)} %select_select_fusion.1), calls=%async_computation.2 | async-start | bytes 4194304 | tf_op jit(solution)/shard_map/all_to_all | solution.py:76
  191.1 35.9 %copy-start.2 = (s32[64]{0:T(128)S(1)}, s32[64]{0:T(128)}, u32[]{:S(2)}) copy-start(s32[64]{0:T(128)} %param.14) | copy-start | bytes 772
  222.4 31.9 %all-to-all-start.4 = ((bf16[16,64,1024]{2,1,0:T(8,128)(2,1)}), bf16[16,64,1024]{2,1,0:T(8,128)(2,1)}, u32[]{:S(2)}, u32[]{:S(2)}) async-start(bf16[16,64,1024]{2,1,0:T(8,128)(2,1)} %bitcast.39), calls=%async_computation.5 | async-start | bytes 4194304 | tf_op jit(solution)/shard_map/all_to_all | solution.py:86
  254.4 32.0 %all-to-all-start.3 = ((bf16[16,64,1024]{2,1,0:T(8,128)(2,1)}), bf16[16,64,1024]{2,1,0:T(8,128)(2,1)}, u32[]{:S(2)}, u32[]{:S(2)}) async-start(bf16[16,64,1024]{2,1,0:T(8,128)(2,1)} %bitcast.40), calls=%async_computation.4 | async-start | bytes 4194304 | tf_op jit(solution)/shard_map/all_to_all | solution.py:105
Sparse Core Ops, SparseCore 0:
  10.4 55.1 reduce-scatter.1
where the time goes:
time: 303 us; the launch traced here: 302 us
  waiting for transfers between devices  97.8 us (32%)
  blocking collectives  89.2 us (29%)
  other arithmetic  36.2 us (12%)
  matrix products  22.9 us (8%)
  local copies, waits for them, and re-layouts  22.7 us (7%)
  starting transfers between devices  18.1 us (6%)
  between operations  14.9 us (5%)
    all_to_all x1, blocking collectives, shards(): lax.all_to_all(pack_slots(second_moment), 'fsdp', split_axis=0, concat_ax...  57.9 us
    all_to_all x1, waiting for transfers between devices, shards(): lax.all_to_all(pack_slots(first_moment), 'fsdp', split_axis=0, concat_axi...  53.3 us
    all_to_all x1, blocking collectives, shards(): lax.all_to_all(as_strips(moment_two).astype(jnp.bfloat16), 'fsdp', split_...  31.3 us
    all_to_all x1, waiting for transfers between devices, shards(): lax.all_to_all(pack_slots(group_sums), 'fsdp', split_axis=0, concat_axis=...  18.1 us
    all_to_all x1, waiting for transfers between devices, shards(): lax.all_to_all(as_strips(moment_one).astype(jnp.bfloat16), 'fsdp', split_...  14.6 us
    gather x3, local copies, waits for them, and re-layouts, pack_slots(): picked = jnp.take(strips, slot_of, axis=0)  12 us
    dot_general x1, matrix products, turn_forward(): return jnp.dot(half_turn, right_matrix, preferred_element_type=jnp.float32)  11.7 us
    dot_general x1, matrix products, turn_back(): lax.dot_general(half_turn, right_matrix, (((1,), (1,)), ((), ())), prefer...  11.2 us
  transfers between devices with their start and end apart: 5, of which 4 were waited for; matrix products, arithmetic and copies ran while one was open for 20% of the time, Pallas kernels for 0%

commit v1 on v0

v1 whole, which is shorter than its diff:
```python
import functools
import math

import jax
import jax.numpy as jnp
from jax import lax
from jax.experimental import pallas as pl
from jax.experimental.pallas import tpu as pltpu
from jax.sharding import PartitionSpec as P

BETA_ONE = 0.9
BETA_TWO = 0.95
EPSILON = 1e-08
MESH = pl.DeviceIdType.MESH
F32 = jnp.float32
BF16 = jnp.bfloat16

NZ = 4
SIDE = 4
NF = SIDE * SIDE
NBD = 8
ROWS = 64
BS = 1024
GROUP = SIDE * ROWS
NCH = 4
CW = BS // NCH
KEEP = 32
BACK = ROWS - KEEP


def new_moments(first, second, rotated):
    moment_one = BETA_ONE * first + (1.0 - BETA_ONE) * rotated
    moment_two = BETA_TWO * second + (1.0 - BETA_TWO) * (rotated * rotated)
    return moment_one, moment_two


def direction_of(moment_one, moment_two, scale_one, scale_two):
    return ((moment_one * scale_one) / (jnp.sqrt(moment_two * scale_two) + EPSILON)).astype(BF16)


def wait_bytes(ref, sem):
    pltpu.make_async_copy(ref, ref, sem).wait()


def kernel(
    owners, counts, part, first, second, left, right,
    out_u, out_m, out_v,
    slot_s, owner_s, scale_one, scale_two,
    own, other, relay_s, relay_r, toward_s, toward_r, summed, grad_s, grad_r,
    lmat, lturn, rmat, half, mom_m, mom_v, ahead_s, ahead_r,
    rot_s, rot_r, dir_s, dir_r, upd_s, upd_r, new_m, new_v, new_u,
    ld_sem, in_sem, core_ss, core_rs, relay_ss, relay_rs, toward_ss, toward_rs,
    grad_ss, grad_rs, ahead_ss, ahead_rs, rot_ss, rot_rs, dir_ss, dir_rs, upd_ss, upd_rs, out_sem,
):
    dp = lax.axis_index("dp")
    me = lax.axis_index("fsdp")
    z, core = dp // 2, dp % 2
    y, x = me // SIDE, me % SIDE
    up, down, far = (z + 1) % NZ, (z + NZ - 1) % NZ, (z + 2) % NZ
    dev_core = (z * 2 + 1 - core, me)
    dev_up = (up * 2 + core, me)
    dev_down = (down * 2 + core, me)

    def peer(index):
        return (dp, index)

    def loop(count, body):
        def step(i, carry):
            body(i)
            return carry

        lax.fori_loop(0, count, step, 0)

    def cols(k):
        return pl.ds(pl.multiple_of(k * CW, CW), CW)

    def load_own(k):
        return pltpu.make_async_copy(part.at[:, core, :, :, cols(k)], own.at[k], ld_sem.at[k])

    in_copies = [
        pltpu.make_async_copy(first, mom_m, in_sem.at[0]),
        pltpu.make_async_copy(second, mom_v, in_sem.at[1]),
        pltpu.make_async_copy(left, lmat, in_sem.at[2]),
        pltpu.make_async_copy(right, rmat, in_sem.at[3]),
    ]
    load_own(0).start()
    load_own(1).start()

    barrier = pltpu.get_barrier_semaphore()
    for device in (dev_core, dev_up, dev_down):
        pl.semaphore_signal(barrier, inc=1, device_id=device, device_id_type=MESH)

    def greet(d):
        pl.semaphore_signal(
            barrier, inc=1, device_id=peer((me + d + 1) % NF), device_id_type=MESH
        )

    loop(NF - 1, greet)

    def find_slots(j):
        slot = jnp.int32(0)
        for b in range(NBD):
            slot = jnp.where(owners[dp * NBD + b] == j, jnp.int32(b), slot)
        slot_s[j] = slot

    loop(NF, find_slots)

    def find_scales(b):
        owner_s[b] = owners[dp * NBD + b]
        count = jnp.full((1, BS), counts[dp * NBD + b].astype(F32), F32)
        scale_one[b] = 1.0 / (1.0 - jnp.exp(count * math.log(BETA_ONE)))
        scale_two[b] = 1.0 / (1.0 - jnp.exp(count * math.log(BETA_TWO)))

    loop(NBD, find_scales)
    pl.semaphore_wait(barrier, NF + 2)

    def send_core(k):
        for zz in (far, up, down, z):
            pltpu.make_async_remote_copy(
                src_ref=part.at[zz, 1 - core, :, :, cols(k)],
                dst_ref=other.at[k, zz],
                send_sem=core_ss,
                recv_sem=core_rs.at[k, zz],
                device_id=dev_core,
                device_id_type=MESH,
            ).start()

    def pair(k, zz, b):
        return own[k, zz, b].astype(F32) + other[k, zz, b].astype(F32)

    def send_toward(k, side, at, device):
        pltpu.make_async_remote_copy(
            src_ref=toward_s.at[k, side, pl.ds(at, NBD // 2)],
            dst_ref=toward_r.at[k, side, pl.ds(at, NBD // 2)],
            send_sem=toward_ss,
            recv_sem=toward_rs.at[k],
            device_id=device,
            device_id_type=MESH,
        ).start()

    hb = NBD // 2

    def sum_far(k):
        load_own(k).wait()
        wait_bytes(other.at[k, far], core_rs.at[k, far])
        for side, device in ((0, dev_up), (1, dev_down)):

            def body(b):
                relay_s[k, side, b] = pair(k, far, side * hb + b).astype(BF16)

            loop(hb, body)
            pltpu.make_async_remote_copy(
                src_ref=relay_s.at[k, side],
                dst_ref=relay_r.at[k, side],
                send_sem=relay_ss,
                recv_sem=relay_rs.at[k, side],
                device_id=device,
                device_id_type=MESH,
            ).start()

    def sum_near(k):
        for side, zz, device in ((0, up, dev_up), (1, down, dev_down)):
            wait_bytes(other.at[k, zz], core_rs.at[k, zz])
            at = (1 - side) * hb

            def body(b):
                toward_s[k, side, at + b] = pair(k, zz, at + b).astype(BF16)

            loop(hb, body)
            send_toward(k, side, at, device)

    def sum_relayed(k):
        for side, zz, device in ((0, up, dev_up), (1, down, dev_down)):
            wait_bytes(relay_r.at[k, side], relay_rs.at[k, side])
            at = side * hb

            def body(b):
                toward_s[k, side, at + b] = (
                    pair(k, zz, at + b) + relay_r[k, side, b].astype(F32)
                ).astype(BF16)

            loop(hb, body)
            send_toward(k, side, at, device)

    def send_grad(k):
        wait_bytes(other.at[k, z], core_rs.at[k, z])
        wait_bytes(toward_r.at[k], toward_rs.at[k])

        def body(b):
            summed[b] = (
                pair(k, z, b) + toward_r[k, 0, b].astype(F32) + toward_r[k, 1, b].astype(F32)
            ).astype(BF16)

        loop(NBD, body)

        def send(d):
            j = (me + d + 1) % NF
            grad_s[k, j] = summed[slot_s[j]]
            pltpu.make_async_remote_copy(
                src_ref=grad_s.at[k, j],
                dst_ref=grad_r.at[k, me],
                send_sem=grad_ss,
                recv_sem=grad_rs.at[k],
                device_id=peer(j),
                device_id_type=MESH,
            ).start()

        loop(NF - 1, send)
        grad_r[k, me] = summed[slot_s[me]]

    def turn_left(k):
        wait_bytes(grad_r.at[k, pl.ds(0, NF - 1)], grad_rs.at[k])

        def body(q):
            rows = pl.ds(pl.multiple_of(q * GROUP, GROUP), GROUP)
            half[rows, cols(k)] = jnp.dot(
                lturn[rows, :], grad_r[k].reshape(BS, CW), preferred_element_type=F32
            ).astype(BF16)

        loop(SIDE, body)

    def send_ahead():
        in_copies[0].wait()
        in_copies[1].wait()

        def send(d):
            j = (me + d) % NF
            slot = slot_s[j]
            ahead_s[j, 0] = mom_m[slot][:KEEP].astype(BF16)
            ahead_s[j, 1] = mom_v[slot][:KEEP].astype(BF16)

            @pl.when(j != me)
            def _():
                pltpu.make_async_remote_copy(
                    src_ref=ahead_s.at[j],
                    dst_ref=ahead_r.at[me],
                    send_sem=ahead_ss,
                    recv_sem=ahead_rs,
                    device_id=peer(j),
                    device_id_type=MESH,
                ).start()

            @pl.when(j == me)
            def _():
                ahead_r[me] = ahead_s[me]

        loop(NF, send)

    def turn_basis():
        in_copies[2].wait()
        in_copies[3].wait()

        def body(q):
            rows = pl.ds(pl.multiple_of(q * GROUP, GROUP), GROUP)
            lturn[rows, :] = lmat[:, rows].T

        loop(SIDE, body)

    def chunk(t):
        @pl.when(t + 2 < NCH)
        def _():
            load_own(t + 2).start()
            send_core(t + 2)

        @pl.when(t < NCH)
        def _():
            sum_far(t)
            sum_near(t)

        @pl.when(t == 0)
        def _():
            send_ahead()
            turn_basis()

        @pl.when((t >= 1) & (t < NCH + 1))
        def _():
            sum_relayed(t - 1)

        @pl.when((t >= 2) & (t < NCH + 2))
        def _():
            send_grad(t - 2)

        @pl.when(t >= 3)
        def _():
            turn_left(t - 3)

    send_core(0)
    send_core(1)
    for copy in in_copies:
        copy.start()
    loop(NCH + 3, chunk)

    my_slot = slot_s[me]
    wait_bytes(ahead_r.at[pl.ds(0, NF - 1)], ahead_rs)

    def turn_right(q):
        yy = (y + 1 + q) % SIDE
        rows = pl.ds(pl.multiple_of(yy * GROUP, GROUP), GROUP)
        rot_s[pl.ds(yy * SIDE, SIDE)] = (
            jnp.dot(half[rows, :], rmat[...], preferred_element_type=F32)
            .astype(BF16)
            .reshape(SIDE, ROWS, BS)
        )

        def send(xx):
            j = yy * SIDE + xx

            @pl.when(j != me)
            def _():
                pltpu.make_async_remote_copy(
                    src_ref=rot_s.at[j],
                    dst_ref=rot_r.at[me],
                    send_sem=rot_ss,
                    recv_sem=rot_rs.at[me],
                    device_id=peer(j),
                    device_id_type=MESH,
                ).start()

            @pl.when(j == me)
            def _():
                rot_r[me] = rot_s[me]

        loop(SIDE, send)

    loop(SIDE, turn_right)

    def direct_ahead(i):
        one, two = scale_one[my_slot], scale_two[my_slot]
        for at in range(0, KEEP, 16):
            rows = pl.ds(at, 16)
            moment_one, moment_two = new_moments(
                ahead_r[i, 0, rows].astype(F32),
                ahead_r[i, 1, rows].astype(F32),
                rot_s[i, rows].astype(F32),
            )
            dir_r[i, rows] = direction_of(moment_one, moment_two, one, two)

    loop(NF, direct_ahead)

    def direct(q):
        jy = (y + 2 * SIDE - 1 - q) % SIDE

        def answer(xx):
            j = jy * SIDE + xx
            slot = slot_s[j]

            @pl.when(j != me)
            def _():
                wait_bytes(rot_r.at[j], rot_rs.at[j])

            one, two = scale_one[slot], scale_two[slot]
            for at in range(0, BACK, 16):
                rows = pl.ds(KEEP + at, 16)
                moment_one, moment_two = new_moments(
                    mom_m[slot, rows], mom_v[slot, rows], rot_r[j, rows].astype(F32)
                )
                dir_s[j, pl.ds(at, 16)] = direction_of(moment_one, moment_two, one, two)

            @pl.when(j != me)
            def _():
                pltpu.make_async_remote_copy(
                    src_ref=dir_s.at[j],
                    dst_ref=dir_r.at[me, pl.ds(KEEP, BACK)],
                    send_sem=dir_ss,
                    recv_sem=dir_rs.at[me],
                    device_id=peer(j),
                    device_id_type=MESH,
                ).start()

            @pl.when(j == me)
            def _():
                dir_r[me, pl.ds(KEEP, BACK)] = dir_s[me]

        loop(SIDE, answer)

    def back_right(q):
        yy = (y + 1 + q) % SIDE

        def arrive(xx):
            i = yy * SIDE + xx

            @pl.when(i != me)
            def _():
                wait_bytes(dir_r.at[i, pl.ds(KEEP, BACK)], dir_rs.at[i])

        loop(SIDE, arrive)
        rows = pl.ds(pl.multiple_of(yy * GROUP, GROUP), GROUP)
        half[rows, :] = lax.dot_general(
            dir_r[pl.ds(yy * SIDE, SIDE)].reshape(GROUP, BS),
            rmat[...],
            (((1,), (1,)), ((), ())),
            preferred_element_type=F32,
        ).astype(BF16)

    def back(q):
        @pl.when(q < SIDE)
        def _():
            direct(q)

        @pl.when(q >= 1)
        def _():
            back_right(q - 1)

    loop(SIDE + 1, back)

    def back_left(q):
        yy = (y + 1 + q) % SIDE
        rows = pl.ds(pl.multiple_of(yy * GROUP, GROUP), GROUP)
        upd_s[pl.ds(yy * SIDE, SIDE)] = (
            jnp.dot(lmat[rows, :], half[...], preferred_element_type=F32)
            .astype(BF16)
            .reshape(SIDE, ROWS, BS)
        )

        def send(xx):
            j = yy * SIDE + xx

            @pl.when(j != me)
            def _():
                pltpu.make_async_remote_copy(
                    src_ref=upd_s.at[j],
                    dst_ref=upd_r.at[me],
                    send_sem=upd_ss,
                    recv_sem=upd_rs,
                    device_id=peer(j),
                    device_id_type=MESH,
                ).start()

            @pl.when(j == me)
            def _():
                upd_r[me] = upd_s[me]

        loop(SIDE, send)

    loop(SIDE, back_left)

    def keep(b):
        owner = owner_s[b]
        for at in range(0, ROWS, 16):
            rows = pl.ds(at, 16)
            new_m[b, rows], new_v[b, rows] = new_moments(
                mom_m[b, rows], mom_v[b, rows], rot_r[owner, rows].astype(F32)
            )

    loop(NBD, keep)
    save_m = pltpu.make_async_copy(new_m, out_m, out_sem.at[0])
    save_v = pltpu.make_async_copy(new_v, out_v, out_sem.at[1])
    save_m.start()
    save_v.start()

    wait_bytes(upd_r.at[pl.ds(0, NF - 1)], upd_rs)

    def take(b):
        new_u[b] = upd_r[owner_s[b]]

    loop(NBD, take)
    save_u = pltpu.make_async_copy(new_u, out_u, out_sem.at[2])
    save_u.start()

    wait_bytes(other, core_ss)
    wait_bytes(relay_s, relay_ss)
    wait_bytes(toward_s, toward_ss)
    wait_bytes(grad_s.at[:, pl.ds(0, NF - 1)], grad_ss)
    wait_bytes(ahead_s.at[pl.ds(0, NF - 1)], ahead_ss)
    wait_bytes(rot_s.at[pl.ds(0, NF - 1)], rot_ss)
    wait_bytes(dir_s.at[pl.ds(0, NF - 1)], dir_ss)
    wait_bytes(upd_s.at[pl.ds(0, NF - 1)], upd_ss)
    save_m.wait()
    save_v.wait()
    save_u.wait()


def shards(partials, first_moment, second_moment, step_counts, owners, left_basis, right_basis):
    part = partials.reshape(NZ, 2, NBD, ROWS, BS)
    strips = (NBD, ROWS, BS)
    slots = (NF, ROWS, BS)
    any_space = pl.BlockSpec(memory_space=pl.ANY)
    scalars = pl.BlockSpec(memory_space=pltpu.SMEM)
    dma = pltpu.SemaphoreType.DMA
    return pl.pallas_call(
        kernel,
        out_shape=(
            jax.ShapeDtypeStruct(strips, BF16),
            jax.ShapeDtypeStruct(strips, F32),
            jax.ShapeDtypeStruct(strips, F32),
        ),
        in_specs=[scalars] * 2 + [any_space] * 5,
        out_specs=(any_space,) * 3,
        scratch_shapes=[
            pltpu.SMEM((NF,), jnp.int32),
            pltpu.SMEM((NBD,), jnp.int32),
            pltpu.VMEM((NBD, 1, BS), F32),
            pltpu.VMEM((NBD, 1, BS), F32),
            pltpu.VMEM((NCH, NZ, NBD, ROWS, CW), BF16),
            pltpu.VMEM((NCH, NZ, NBD, ROWS, CW), BF16),
            pltpu.VMEM((NCH, 2, NBD // 2, ROWS, CW), BF16),
            pltpu.VMEM((NCH, 2, NBD // 2, ROWS, CW), BF16),
            pltpu.VMEM((NCH, 2, NBD, ROWS, CW), BF16),
            pltpu.VMEM((NCH, 2, NBD, ROWS, CW), BF16),
            pltpu.VMEM((NBD, ROWS, CW), BF16),
            pltpu.VMEM((NCH, NF, ROWS, CW), BF16),
            pltpu.VMEM((NCH, NF, ROWS, CW), BF16),
            pltpu.VMEM((BS, BS), BF16),
            pltpu.VMEM((BS, BS), BF16),
            pltpu.VMEM((BS, BS), BF16),
            pltpu.VMEM((BS, BS), BF16),
            pltpu.VMEM(strips, F32),
            pltpu.VMEM(strips, F32),
            pltpu.VMEM((NF, 2, KEEP, BS), BF16),
            pltpu.VMEM((NF, 2, KEEP, BS), BF16),
            pltpu.VMEM(slots, BF16),
            pltpu.VMEM(slots, BF16),
            pltpu.VMEM((NF, BACK, BS), BF16),
            pltpu.VMEM(slots, BF16),
            pltpu.VMEM(slots, BF16),
            pltpu.VMEM(slots, BF16),
            pltpu.VMEM(strips, F32),
            pltpu.VMEM(strips, F32),
            pltpu.VMEM(strips, BF16),
            dma((NCH,)),
            dma((4,)),
            dma,
            dma((NCH, NZ)),
            dma,
            dma((NCH, 2)),
            dma,
            dma((NCH,)),
            dma,
            dma((NCH,)),
            dma,
            dma,
            dma,
            dma((NF,)),
            dma,
            dma((NF,)),
            dma,
            dma,
            dma((3,)),
        ],
        compiler_params=pltpu.CompilerParams(
            collective_id=0, has_side_effects=True, vmem_limit_bytes=60 * 2**20
        ),
        name="soap_step",
    )(owners, step_counts, part, first_moment, second_moment, left_basis[0, 0], right_basis[0, 0])


def solution(mesh):
    placed = (
        P("dp", None, "fsdp", None),
        P("dp", "fsdp", None),
        P("dp", "fsdp", None),
        P(),
        P(),
        P("dp", "fsdp", None, None),
        P("dp", "fsdp", None, None),
    )
    return jax.shard_map(
        shards,
        mesh=mesh,
        in_specs=placed,
        out_specs=(P("dp", "fsdp", None), P("dp", "fsdp", None), P("dp", "fsdp", None)),
        check_vma=False,
    )
```

time: 303 us -> 154 us (0.51)
  the two profiles are of different devices: /device:TPU:0 before, /device:TPU:28 now
where the time goes in v1:
time: 154 us
  Pallas kernels  147 us (95%)
  local copies, waits for them, and re-layouts  6.08 us (4%)
    pallas_call x1, Pallas kernels, shards(): pl.pallas_call(kernel, out_shape=(jax.ShapeDtypeStruct(strips, BF16), jax...  147 us
    unnamed x7, local copies, waits for them, and re-layouts  6.08 us

profile of v1, /device:TPU:28, one launch (start us, length us, event | category | flops | bytes accessed | tf_op | source)
XLA Modules:
  0.0 154.0 jit_solution(322723469758634437)
XLA Ops:
  0.6 147.2 %soap_step.1 = (bf16[8,64,1024]{2,1,0:T(8,128)(2,1)}, f32[8,64,1024]{2,1,0:T(8,128)}, f32[8,64,1024]{2,1,0:T(8,128)}) custom-call(s32[64]{0:T(128)} %owners.1, s32[64]{0:T(128)} %counts.1, bf16[4,2,8,64,1024]{4,3,2,1,0:T(8,128)(2,1)} %bitcast.3, f32[8,64,1024]{2,1,0:T(8,128)} %first.1, f32[8,64,1024]{2,1,0:T(8,128)} %second.1, bf16[1024,1024]{1,0:T(8,128)(2,1)} %bitcast.4, ...), custom_call_target="tpu_custom_call" | custom-call | tf_op jit(solution)/shard_map/soap_step/pallas_call | solution.py:480
  147.9 0.0 copy-start.1
  147.9 2.4 %copy.13 = bf16[8,64,1024]{2,1,0:T(8,128)(2,1)} copy(bf16[8,64,1024]{2,1,0:T(8,128)(2,1)} %get-tuple-element.6) | data formatting | bytes 2097152
  150.3 0.0 copy-done.1
  150.3 0.0 copy-start
  150.3 1.3 copy.14
  151.6 1.0 copy-done
  152.7 1.3 copy.15
Async XLA Ops:
  147.9 2.4 %copy-start.1 = (f32[8,64,1024]{2,1,0:T(8,128)S(1)}, f32[8,64,1024]{2,1,0:T(8,128)}, u32[]{:S(2)}) copy-start(f32[8,64,1024]{2,1,0:T(8,128)} %get-tuple-element.7) | copy-start | bytes 6291460
  150.3 2.3 %copy-start = (f32[8,64,1024]{2,1,0:T(8,128)S(1)}, f32[8,64,1024]{2,1,0:T(8,128)}, u32[]{:S(2)}) copy-start(f32[8,64,1024]{2,1,0:T(8,128)} %get-tuple-element.8) | copy-start | bytes 6291460

commit v2 on v1

--- a/solution.py
+++ b/solution.py
@@ -22,10 +22,20 @@
 ROWS = 64
 BS = 1024
 GROUP = SIDE * ROWS
-NCH = 4
+NCH = 8
 CW = BS // NCH
-KEEP = 32
+PAIR = 2
+KEEP = 16
 BACK = ROWS - KEEP
+PIECE = ROWS // 2
+TURNS = (2, 1, 3, 0)
+PARTS = (
+    ((2, 2), (2, 1), (2, 3)),
+    ((1, 2), (1, 1), (1, 3)),
+    ((3, 2), (3, 3), (3, 1), (2, 0)),
+    ((0, 2), (1, 0), (3, 0), (0, 1), (0, 3)),
+)
+ORDER = sum(PARTS, ())
 
 
 def new_moments(first, second, rotated):
@@ -44,13 +54,13 @@
 
 def kernel(
     owners, counts, part, first, second, left, right,
-    out_u, out_m, out_v,
+    rot_o, upd_r,
     slot_s, owner_s, scale_one, scale_two,
     own, other, relay_s, relay_r, toward_s, toward_r, summed, grad_s, grad_r,
     lmat, lturn, rmat, half, mom_m, mom_v, ahead_s, ahead_r,
-    rot_s, rot_r, dir_s, dir_r, upd_s, upd_r, new_m, new_v, new_u,
+    rot_s, rot_r, dir_s, dir_r, upd_s, strips,
     ld_sem, in_sem, core_ss, core_rs, relay_ss, relay_rs, toward_ss, toward_rs,
-    grad_ss, grad_rs, ahead_ss, ahead_rs, rot_ss, rot_rs, dir_ss, dir_rs, upd_ss, upd_rs, out_sem,
+    grad_ss, grad_rs, ahead_ss, ahead_rs, rot_ss, rot_rs, kept_ss, kept_rs, dir_ss, dir_rs, upd_ss, upd_rs, out_sem,
 ):
     dp = lax.axis_index("dp")
     me = lax.axis_index("fsdp")
@@ -70,6 +80,32 @@
             return carry
 
         lax.fori_loop(0, count, step, 0)
+
+    def chosen(n, values):
+        value = jnp.int32(values[0])
+        for i, other_value in enumerate(values[1:]):
+            value = jnp.where(n == i + 1, jnp.int32(other_value), value)
+        return value
+
+    def to_nth(n):
+        yy = (y + chosen(n, [dy for dy, _ in ORDER])) % SIDE
+        return yy * SIDE + (x + chosen(n, [dx for _, dx in ORDER])) % SIDE
+
+    def from_nth(n):
+        yy = (y + SIDE - chosen(n, [dy for dy, _ in ORDER])) % SIDE
+        return yy * SIDE + (x + SIDE - chosen(n, [dx for _, dx in ORDER])) % SIDE
+
+    def send_part(n, send):
+        for i, part_n in enumerate(PARTS):
+
+            @pl.when(n == i)
+            def _():
+                for dy, dx in part_n:
+                    send(((y + dy) % SIDE) * SIDE + (x + dx) % SIDE)
+
+    def turn_rows(n):
+        yy = (y + chosen(n, TURNS)) % SIDE
+        return yy, pl.ds(pl.multiple_of(yy * GROUP, GROUP), GROUP)
 
     def cols(k):
         return pl.ds(pl.multiple_of(k * CW, CW), CW)
@@ -193,8 +229,8 @@
 
         loop(NBD, body)
 
-        def send(d):
-            j = (me + d + 1) % NF
+        def send(n):
+            j = to_nth(n)
             grad_s[k, j] = summed[slot_s[j]]
             pltpu.make_async_remote_copy(
                 src_ref=grad_s.at[k, j],
@@ -208,13 +244,16 @@
         loop(NF - 1, send)
         grad_r[k, me] = summed[slot_s[me]]
 
-    def turn_left(k):
-        wait_bytes(grad_r.at[k, pl.ds(0, NF - 1)], grad_rs.at[k])
+    def turn_left(p):
+        k = PAIR * p
+        for n in range(PAIR):
+            wait_bytes(grad_r.at[k + n, pl.ds(0, NF - 1)], grad_rs.at[k + n])
 
         def body(q):
             rows = pl.ds(pl.multiple_of(q * GROUP, GROUP), GROUP)
-            half[rows, cols(k)] = jnp.dot(
-                lturn[rows, :], grad_r[k].reshape(BS, CW), preferred_element_type=F32
+            grad = jnp.concatenate([grad_r[k + n].reshape(BS, CW) for n in range(PAIR)], axis=1)
+            half[rows, pl.ds(pl.multiple_of(k * CW, PAIR * CW), PAIR * CW)] = jnp.dot(
+                lturn[rows, :], grad, preferred_element_type=F32
             ).astype(BF16)
 
         loop(SIDE, body)
@@ -223,28 +262,26 @@
         in_copies[0].wait()
         in_copies[1].wait()
 
-        def send(d):
-            j = (me + d) % NF
+        def pack(j):
             slot = slot_s[j]
             ahead_s[j, 0] = mom_m[slot][:KEEP].astype(BF16)
             ahead_s[j, 1] = mom_v[slot][:KEEP].astype(BF16)
 
-            @pl.when(j != me)
-            def _():
-                pltpu.make_async_remote_copy(
-                    src_ref=ahead_s.at[j],
-                    dst_ref=ahead_r.at[me],
-                    send_sem=ahead_ss,
-                    recv_sem=ahead_rs,
-                    device_id=peer(j),
-                    device_id_type=MESH,
-                ).start()
-
-            @pl.when(j == me)
-            def _():
-                ahead_r[me] = ahead_s[me]
-
-        loop(NF, send)
+        def send(n):
+            j = to_nth(n)
+            pack(j)
+            pltpu.make_async_remote_copy(
+                src_ref=ahead_s.at[j],
+                dst_ref=ahead_r.at[me],
+                send_sem=ahead_ss,
+                recv_sem=ahead_rs,
+                device_id=peer(j),
+                device_id_type=MESH,
+            ).start()
+
+        loop(NF - 1, send)
+        pack(me)
+        ahead_r[me] = ahead_s[me]
 
     def turn_basis():
         in_copies[2].wait()
@@ -276,53 +313,52 @@
         def _():
             sum_relayed(t - 1)
 
-        @pl.when((t >= 2) & (t < NCH + 2))
+        @pl.when(t >= 2)
         def _():
             send_grad(t - 2)
-
-        @pl.when(t >= 3)
-        def _():
-            turn_left(t - 3)
 
     send_core(0)
     send_core(1)
     for copy in in_copies:
         copy.start()
-    loop(NCH + 3, chunk)
+    loop(NCH + 2, chunk)
+    loop(NCH // PAIR, turn_left)
 
     my_slot = slot_s[me]
     wait_bytes(ahead_r.at[pl.ds(0, NF - 1)], ahead_rs)
 
-    def turn_right(q):
-        yy = (y + 1 + q) % SIDE
-        rows = pl.ds(pl.multiple_of(yy * GROUP, GROUP), GROUP)
+    def send_rotated(j):
+        pltpu.make_async_remote_copy(
+            src_ref=rot_s.at[j, pl.ds(KEEP, BACK)],
+            dst_ref=rot_r.at[me, pl.ds(KEEP, BACK)],
+            send_sem=rot_ss,
+            recv_sem=rot_rs.at[me],
+            device_id=peer(j),
+            device_id_type=MESH,
+        ).start()
+
+    def send_kept(n):
+        j = to_nth(n)
+        pltpu.make_async_remote_copy(
+            src_ref=rot_s.at[j, pl.ds(0, KEEP)],
+            dst_ref=rot_r.at[me, pl.ds(0, KEEP)],
+            send_sem=kept_ss,
+            recv_sem=kept_rs,
+            device_id=peer(j),
+            device_id_type=MESH,
+        ).start()
+
+    def turn_right(n):
+        yy, rows = turn_rows(n)
         rot_s[pl.ds(yy * SIDE, SIDE)] = (
             jnp.dot(half[rows, :], rmat[...], preferred_element_type=F32)
             .astype(BF16)
             .reshape(SIDE, ROWS, BS)
         )
-
-        def send(xx):
-            j = yy * SIDE + xx
-
-            @pl.when(j != me)
-            def _():
-                pltpu.make_async_remote_copy(
-                    src_ref=rot_s.at[j],
-                    dst_ref=rot_r.at[me],
-                    send_sem=rot_ss,
-                    recv_sem=rot_rs.at[me],
-                    device_id=peer(j),
-                    device_id_type=MESH,
-                ).start()
-
-            @pl.when(j == me)
-            def _():
-                rot_r[me] = rot_s[me]
-
-        loop(SIDE, send)
+        send_part(n, send_rotated)
 
     loop(SIDE, turn_right)
+    rot_r[me] = rot_s[me]
 
     def direct_ahead(i):
         one, two = scale_one[my_slot], scale_two[my_slot]
@@ -337,44 +373,36 @@
 
     loop(NF, direct_ahead)
 
-    def direct(q):
-        jy = (y + 2 * SIDE - 1 - q) % SIDE
-
-        def answer(xx):
-            j = jy * SIDE + xx
-            slot = slot_s[j]
-
-            @pl.when(j != me)
-            def _():
-                wait_bytes(rot_r.at[j], rot_rs.at[j])
-
-            one, two = scale_one[slot], scale_two[slot]
-            for at in range(0, BACK, 16):
-                rows = pl.ds(KEEP + at, 16)
-                moment_one, moment_two = new_moments(
-                    mom_m[slot, rows], mom_v[slot, rows], rot_r[j, rows].astype(F32)
-                )
-                dir_s[j, pl.ds(at, 16)] = direction_of(moment_one, moment_two, one, two)
-
-            @pl.when(j != me)
-            def _():
-                pltpu.make_async_remote_copy(
-                    src_ref=dir_s.at[j],
-                    dst_ref=dir_r.at[me, pl.ds(KEEP, BACK)],
-                    send_sem=dir_ss,
-                    recv_sem=dir_rs.at[me],
-                    device_id=peer(j),
-                    device_id_type=MESH,
-                ).start()
-
-            @pl.when(j == me)
-            def _():
-                dir_r[me, pl.ds(KEEP, BACK)] = dir_s[me]
-
-        loop(SIDE, answer)
-
-    def back_right(q):
-        yy = (y + 1 + q) % SIDE
+    def direct(j):
+        slot = slot_s[j]
+        one, two = scale_one[slot], scale_two[slot]
+        for at in range(0, BACK, 16):
+            rows = pl.ds(KEEP + at, 16)
+            moment_one, moment_two = new_moments(
+                mom_m[slot, rows], mom_v[slot, rows], rot_r[j, rows].astype(F32)
+            )
+            dir_s[j, pl.ds(at, 16)] = direction_of(moment_one, moment_two, one, two)
+
+    def answer(n):
+        j = from_nth(n)
+        wait_bytes(rot_r.at[j, pl.ds(KEEP, BACK)], rot_rs.at[j])
+        direct(j)
+        pltpu.make_async_remote_copy(
+            src_ref=dir_s.at[j],
+            dst_ref=dir_r.at[me, pl.ds(KEEP, BACK)],
+            send_sem=dir_ss,
+            recv_sem=dir_rs.at[me],
+            device_id=peer(j),
+            device_id_type=MESH,
+        ).start()
+
+    loop(NF - 1, answer)
+    loop(NF - 1, send_kept)
+    direct(me)
+    dir_r[me, pl.ds(KEEP, BACK)] = dir_s[me]
+
+    def back_right(n):
+        yy, rows = turn_rows(n)
 
         def arrive(xx):
             i = yy * SIDE + xx
@@ -384,7 +412,6 @@
                 wait_bytes(dir_r.at[i, pl.ds(KEEP, BACK)], dir_rs.at[i])
 
         loop(SIDE, arrive)
-        rows = pl.ds(pl.multiple_of(yy * GROUP, GROUP), GROUP)
         half[rows, :] = lax.dot_general(
             dir_r[pl.ds(yy * SIDE, SIDE)].reshape(GROUP, BS),
             rmat[...],
@@ -392,82 +419,90 @@
             preferred_element_type=F32,
         ).astype(BF16)
 
-    def back(q):
-        @pl.when(q < SIDE)
-        def _():
-            direct(q)
-
-        @pl.when(q >= 1)
-        def _():
-            back_right(q - 1)
-
-    loop(SIDE + 1, back)
-
-    def back_left(q):
-        yy = (y + 1 + q) % SIDE
-        rows = pl.ds(pl.multiple_of(yy * GROUP, GROUP), GROUP)
+    loop(SIDE, back_right)
+
+    def send_update(j, at):
+        pltpu.make_async_remote_copy(
+            src_ref=upd_s.at[j, pl.ds(at, PIECE)],
+            dst_ref=upd_r.at[me, pl.ds(at, PIECE)],
+            send_sem=upd_ss,
+            recv_sem=upd_rs,
+            device_id=peer(j),
+            device_id_type=MESH,
+        ).start()
+
+    def back_left(n):
+        yy, rows = turn_rows(n)
         upd_s[pl.ds(yy * SIDE, SIDE)] = (
             jnp.dot(lmat[rows, :], half[...], preferred_element_type=F32)
             .astype(BF16)
             .reshape(SIDE, ROWS, BS)
         )
-
-        def send(xx):
-            j = yy * SIDE + xx
-
-            @pl.when(j != me)
-            def _():
-                pltpu.make_async_remote_copy(
-                    src_ref=upd_s.at[j],
-                    dst_ref=upd_r.at[me],
-                    send_sem=upd_ss,
-                    recv_sem=upd_rs,
-                    device_id=peer(j),
-                    device_id_type=MESH,
-                ).start()
-
-            @pl.when(j == me)
-            def _():
-                upd_r[me] = upd_s[me]
-
-        loop(SIDE, send)
+        send_part(n, lambda j: send_update(j, 0))
 
     loop(SIDE, back_left)
-
-    def keep(b):
-        owner = owner_s[b]
-        for at in range(0, ROWS, 16):
-            rows = pl.ds(at, 16)
-            new_m[b, rows], new_v[b, rows] = new_moments(
-                mom_m[b, rows], mom_v[b, rows], rot_r[owner, rows].astype(F32)
-            )
-
-    loop(NBD, keep)
-    save_m = pltpu.make_async_copy(new_m, out_m, out_sem.at[0])
-    save_v = pltpu.make_async_copy(new_v, out_v, out_sem.at[1])
-    save_m.start()
-    save_v.start()
-
-    wait_bytes(upd_r.at[pl.ds(0, NF - 1)], upd_rs)
+    loop(NF - 1, lambda n: send_update(to_nth(n), PIECE))
+    save_own = pltpu.make_async_copy(upd_s.at[me], upd_r.at[me], out_sem.at[1])
+    save_own.start()
+
+    wait_bytes(rot_r.at[pl.ds(0, NF - 1), pl.ds(0, KEEP)], kept_rs)
 
     def take(b):
-        new_u[b] = upd_r[owner_s[b]]
+        strips[b] = rot_r[owner_s[b]]
 
     loop(NBD, take)
-    save_u = pltpu.make_async_copy(new_u, out_u, out_sem.at[2])
-    save_u.start()
+    save = pltpu.make_async_copy(strips, rot_o, out_sem.at[0])
+    save.start()
+    wait_bytes(upd_s.at[pl.ds(0, NF - 1)], upd_rs)
 
     wait_bytes(other, core_ss)
     wait_bytes(relay_s, relay_ss)
     wait_bytes(toward_s, toward_ss)
     wait_bytes(grad_s.at[:, pl.ds(0, NF - 1)], grad_ss)
     wait_bytes(ahead_s.at[pl.ds(0, NF - 1)], ahead_ss)
-    wait_bytes(rot_s.at[pl.ds(0, NF - 1)], rot_ss)
+    wait_bytes(rot_s.at[pl.ds(0, NF - 1), pl.ds(KEEP, BACK)], rot_ss)
+    wait_bytes(rot_s.at[pl.ds(0, NF - 1), pl.ds(0, KEEP)], kept_ss)
     wait_bytes(dir_s.at[pl.ds(0, NF - 1)], dir_ss)
     wait_bytes(upd_s.at[pl.ds(0, NF - 1)], upd_ss)
-    save_m.wait()
-    save_v.wait()
-    save_u.wait()
+    save.wait()
+    save_own.wait()
+
+
+def keep_kernel(
+    owners, rot, upd, first, second, out_u, out_m, out_v,
+    mom_m, mom_v, rows_r, rows_u, new_m, new_v, in_sem, out_sem,
+):
+    base = lax.axis_index("dp") * NBD
+    copies = []
+    for b in range(NBD):
+        copies.append(
+            [
+                pltpu.make_async_copy(first.at[b], mom_m.at[b], in_sem.at[b, 0]),
+                pltpu.make_async_copy(second.at[b], mom_v.at[b], in_sem.at[b, 1]),
+                pltpu.make_async_copy(rot.at[b], rows_r.at[b], in_sem.at[b, 2]),
+                pltpu.make_async_copy(upd.at[owners[base + b]], rows_u.at[b], in_sem.at[b, 3]),
+            ]
+        )
+        for copy in copies[b]:
+            copy.start()
+    saves = []
+    for b in range(NBD):
+        for copy in copies[b]:
+            copy.wait()
+
+        def step(i, carry, b=b):
+            rows = pl.ds(pl.multiple_of(i * 16, 16), 16)
+            new_m[b, rows], new_v[b, rows] = new_moments(
+                mom_m[b, rows], mom_v[b, rows], rows_r[b, rows].astype(F32)
+            )
+            return carry
+
+        lax.fori_loop(0, ROWS // 16, step, 0)
+        for n, (source, target) in enumerate(((rows_u, out_u), (new_m, out_m), (new_v, out_v))):
+            saves.append(pltpu.make_async_copy(source.at[b], target.at[b], out_sem.at[b, n]))
+            saves[-1].start()
+    for save in saves:
+        save.wait()
 
 
 def shards(partials, first_moment, second_moment, step_counts, owners, left_basis, right_basis):
@@ -477,15 +512,11 @@
     any_space = pl.BlockSpec(memory_space=pl.ANY)
     scalars = pl.BlockSpec(memory_space=pltpu.SMEM)
     dma = pltpu.SemaphoreType.DMA
-    return pl.pallas_call(
+    rotated, update = pl.pallas_call(
         kernel,
-        out_shape=(
-            jax.ShapeDtypeStruct(strips, BF16),
-            jax.ShapeDtypeStruct(strips, F32),
-            jax.ShapeDtypeStruct(strips, F32),
-        ),
+        out_shape=(jax.ShapeDtypeStruct(strips, BF16), jax.ShapeDtypeStruct(slots, BF16)),
         in_specs=[scalars] * 2 + [any_space] * 5,
-        out_specs=(any_space,) * 3,
+        out_specs=(any_space,) * 2,
         scratch_shapes=[
             pltpu.SMEM((NF,), jnp.int32),
             pltpu.SMEM((NBD,), jnp.int32),
@@ -513,9 +544,6 @@
             pltpu.VMEM((NF, BACK, BS), BF16),
             pltpu.VMEM(slots, BF16),
             pltpu.VMEM(slots, BF16),
-            pltpu.VMEM(slots, BF16),
-            pltpu.VMEM(strips, F32),
-            pltpu.VMEM(strips, F32),
             pltpu.VMEM(strips, BF16),
             dma((NCH,)),
             dma((4,)),
@@ -532,16 +560,40 @@
             dma,
             dma((NF,)),
             dma,
+            dma,
+            dma,
             dma((NF,)),
             dma,
             dma,
-            dma((3,)),
+            dma((2,)),
         ],
         compiler_params=pltpu.CompilerParams(
             collective_id=0, has_side_effects=True, vmem_limit_bytes=60 * 2**20
         ),
         name="soap_step",
     )(owners, step_counts, part, first_moment, second_moment, left_basis[0, 0], right_basis[0, 0])
+    return pl.pallas_call(
+        keep_kernel,
+        out_shape=(
+            jax.ShapeDtypeStruct(strips, BF16),
+            jax.ShapeDtypeStruct(strips, F32),
+            jax.ShapeDtypeStruct(strips, F32),
+        ),
+        in_specs=[scalars] + [any_space] * 4,
+        out_specs=(any_space,) * 3,
+        scratch_shapes=[
+            pltpu.VMEM(strips, F32),
+            pltpu.VMEM(strips, F32),
+            pltpu.VMEM(strips, BF16),
+            pltpu.VMEM(strips, BF16),
+            pltpu.VMEM(strips, F32),
+            pltpu.VMEM(strips, F32),
+            dma((NBD, 4)),
+            dma((NBD, 3)),
+        ],
+        compiler_params=pltpu.CompilerParams(vmem_limit_bytes=60 * 2**20),
+        name="keep_moments",
+    )(owners, rotated, update, first_moment, second_moment)
 
 
 def solution(mesh):

time: 154 us -> 130 us (0.84)
  the two profiles are of different devices: /device:TPU:28 before, /device:TPU:0 now
where the time goes in v2:
time: 130 us
  Pallas kernels  129 us (99%)
    pallas_call x1, Pallas kernels, shards(): pl.pallas_call(kernel, out_shape=(jax.ShapeDtypeStruct(strips, BF16), jax...  123 us
    pallas_call x1, Pallas kernels, shards(): pl.pallas_call(keep_kernel, out_shape=(jax.ShapeDtypeStruct(strips, BF16)...  6.22 us

profile of v2, /device:TPU:0, one launch (start us, length us, event | category | flops | bytes accessed | tf_op | source)
XLA Modules:
  0.0 129.8 jit_solution(16296403917012544117)
XLA Ops:
  0.6 122.9 %soap_step.1 = (bf16[8,64,1024]{2,1,0:T(8,128)(2,1)}, bf16[16,64,1024]{2,1,0:T(8,128)(2,1)}) custom-call(s32[64]{0:T(128)} %owners.3, s32[64]{0:T(128)} %counts.1, bf16[4,2,8,64,1024]{4,3,2,1,0:T(8,128)(2,1)} %bitcast.3, f32[8,64,1024]{2,1,0:T(8,128)} %first.3, f32[8,64,1024]{2,1,0:T(8,128)} %second.3, bf16[1024,1024]{1,0:T(8,128)(2,1)} %bitcast.4, ...), custom_call_target="tpu_custom_call" | custom-call | tf_op jit(solution)/shard_map/soap_step/pallas_call | solution.py:515
  123.6 6.2 %keep_moments.1 = (bf16[8,64,1024]{2,1,0:T(8,128)(2,1)}, f32[8,64,1024]{2,1,0:T(8,128)}, f32[8,64,1024]{2,1,0:T(8,128)}) custom-call(s32[64]{0:T(128)} %owners.3, bf16[8,64,1024]{2,1,0:T(8,128)(2,1)} %get-tuple-element.5.rot, bf16[16,64,1024]{2,1,0:T(8,128)(2,1)} %get-tuple-element.6.upd, f32[8,64,1024]{2,1,0:T(8,128)} %first.3, f32[8,64,1024]{2,1,0:T(8,128)} %second.3), custom_call_target="tpu_custom_call" | custom-call | tf_op jit(solution)/shard_map/keep_moments/pallas_call | solution.py:575

commit v3 on v2

--- a/solution.py
+++ b/solution.py
@@ -25,8 +25,10 @@
 NCH = 8
 CW = BS // NCH
 PAIR = 2
+FIRST = BS - PAIR * CW
 KEEP = 16
 BACK = ROWS - KEEP
+SLICE = 16
 PIECE = ROWS // 2
 TURNS = (2, 1, 3, 0)
 PARTS = (
@@ -54,13 +56,13 @@
 
 def kernel(
     owners, counts, part, first, second, left, right,
-    rot_o, upd_r,
+    out_u, out_m, out_v,
     slot_s, owner_s, scale_one, scale_two,
     own, other, relay_s, relay_r, toward_s, toward_r, summed, grad_s, grad_r,
-    lmat, lturn, rmat, half, mom_m, mom_v, ahead_s, ahead_r,
-    rot_s, rot_r, dir_s, dir_r, upd_s, strips,
+    lmat, lturn, rmat, half, begun, mom_m, mom_v, ahead_s, ahead_r,
+    rot_s, rot_r, dir_s, dir_r, upd_s, upd_r,
     ld_sem, in_sem, core_ss, core_rs, relay_ss, relay_rs, toward_ss, toward_rs,
-    grad_ss, grad_rs, ahead_ss, ahead_rs, rot_ss, rot_rs, kept_ss, kept_rs, dir_ss, dir_rs, upd_ss, upd_rs, out_sem,
+    grad_ss, grad_rs, ahead_ss, ahead_rs, rot_ss, rot_rs, kept_ss, kept_rs, dir_ss, dir_rs, upd_ss, upd_rs,
 ):
     dp = lax.axis_index("dp")
     me = lax.axis_index("fsdp")
@@ -322,17 +324,25 @@
     for copy in in_copies:
         copy.start()
     loop(NCH + 2, chunk)
-    loop(NCH // PAIR, turn_left)
+    loop(NCH // PAIR - 1, turn_left)
+
+    def begin(q):
+        rows = pl.ds(pl.multiple_of(q * GROUP, GROUP), GROUP)
+        begun[rows, :] = jnp.dot(half[rows, :FIRST], rmat[:FIRST, :], preferred_element_type=F32)
+
+    loop(SIDE, begin)
+    turn_left(NCH // PAIR - 1)
 
     my_slot = slot_s[me]
     wait_bytes(ahead_r.at[pl.ds(0, NF - 1)], ahead_rs)
 
-    def send_rotated(j):
+    def send_rotated(j, r):
+        rows = pl.ds(KEEP + r * SLICE, SLICE)
         pltpu.make_async_remote_copy(
-            src_ref=rot_s.at[j, pl.ds(KEEP, BACK)],
-            dst_ref=rot_r.at[me, pl.ds(KEEP, BACK)],
+            src_ref=rot_s.at[j, rows],
+            dst_ref=rot_r.at[me, rows],
             send_sem=rot_ss,
-            recv_sem=rot_rs.at[me],
+            recv_sem=rot_rs.at[r, me],
             device_id=peer(j),
             device_id_type=MESH,
         ).start()
@@ -351,13 +361,15 @@
     def turn_right(n):
         yy, rows = turn_rows(n)
         rot_s[pl.ds(yy * SIDE, SIDE)] = (
-            jnp.dot(half[rows, :], rmat[...], preferred_element_type=F32)
+            (begun[rows, :] + jnp.dot(half[rows, FIRST:], rmat[FIRST:, :], preferred_element_type=F32))
             .astype(BF16)
             .reshape(SIDE, ROWS, BS)
         )
-        send_part(n, send_rotated)
+        send_part(n, lambda j: send_rotated(j, 0))
 
     loop(SIDE, turn_right)
+    for r in range(1, BACK // SLICE):
+        loop(NF - 1, lambda n, r=r: send_rotated(to_nth(n), r))
     rot_r[me] = rot_s[me]
 
     def direct_ahead(i):
@@ -373,32 +385,35 @@
 
     loop(NF, direct_ahead)
 
-    def direct(j):
+    def direct(j, r):
         slot = slot_s[j]
-        one, two = scale_one[slot], scale_two[slot]
-        for at in range(0, BACK, 16):
-            rows = pl.ds(KEEP + at, 16)
-            moment_one, moment_two = new_moments(
-                mom_m[slot, rows], mom_v[slot, rows], rot_r[j, rows].astype(F32)
-            )
-            dir_s[j, pl.ds(at, 16)] = direction_of(moment_one, moment_two, one, two)
-
-    def answer(n):
+        rows = pl.ds(KEEP + r * SLICE, SLICE)
+        moment_one, moment_two = new_moments(
+            mom_m[slot, rows], mom_v[slot, rows], rot_r[j, rows].astype(F32)
+        )
+        dir_s[j, pl.ds(r * SLICE, SLICE)] = direction_of(
+            moment_one, moment_two, scale_one[slot], scale_two[slot]
+        )
+
+    def answer(n, r):
         j = from_nth(n)
-        wait_bytes(rot_r.at[j, pl.ds(KEEP, BACK)], rot_rs.at[j])
-        direct(j)
+        rows = pl.ds(KEEP + r * SLICE, SLICE)
+        wait_bytes(rot_r.at[j, rows], rot_rs.at[r, j])
+        direct(j, r)
         pltpu.make_async_remote_copy(
-            src_ref=dir_s.at[j],
-            dst_ref=dir_r.at[me, pl.ds(KEEP, BACK)],
+            src_ref=dir_s.at[j, pl.ds(r * SLICE, SLICE)],
+            dst_ref=dir_r.at[me, rows],
             send_sem=dir_ss,
             recv_sem=dir_rs.at[me],
             device_id=peer(j),
             device_id_type=MESH,
         ).start()
 
-    loop(NF - 1, answer)
+    for r in range(BACK // SLICE):
+        loop(NF - 1, lambda n, r=r: answer(n, r))
     loop(NF - 1, send_kept)
-    direct(me)
+    for r in range(BACK // SLICE):
+        direct(me, r)
     dir_r[me, pl.ds(KEEP, BACK)] = dir_s[me]
 
     def back_right(n):
@@ -419,7 +434,19 @@
             preferred_element_type=F32,
         ).astype(BF16)
 
-    loop(SIDE, back_right)
+    loop(SIDE - 1, back_right)
+
+    def begin_left(q):
+        rows = pl.ds(pl.multiple_of(q * GROUP, GROUP), GROUP)
+        total = None
+        for n in range(SIDE - 1):
+            _, used = turn_rows(n)
+            part_n = jnp.dot(lmat[rows, used], half[used, :], preferred_element_type=F32)
+            total = part_n if total is None else total + part_n
+        begun[rows, :] = total
+
+    loop(SIDE, begin_left)
+    back_right(SIDE - 1)
 
     def send_update(j, at):
         pltpu.make_async_remote_copy(
@@ -433,8 +460,9 @@
 
     def back_left(n):
         yy, rows = turn_rows(n)
+        _, last = turn_rows(SIDE - 1)
         upd_s[pl.ds(yy * SIDE, SIDE)] = (
-            jnp.dot(lmat[rows, :], half[...], preferred_element_type=F32)
+            (begun[rows, :] + jnp.dot(lmat[rows, last], half[last, :], preferred_element_type=F32))
             .astype(BF16)
             .reshape(SIDE, ROWS, BS)
         )
@@ -442,18 +470,25 @@
 
     loop(SIDE, back_left)
     loop(NF - 1, lambda n: send_update(to_nth(n), PIECE))
-    save_own = pltpu.make_async_copy(upd_s.at[me], upd_r.at[me], out_sem.at[1])
-    save_own.start()
+    upd_r[me] = upd_s[me]
 
     wait_bytes(rot_r.at[pl.ds(0, NF - 1), pl.ds(0, KEEP)], kept_rs)
 
+    def keep(b):
+        owner = owner_s[b]
+        for at in range(0, ROWS, SLICE):
+            rows = pl.ds(at, SLICE)
+            out_m[b, rows], out_v[b, rows] = new_moments(
+                mom_m[b, rows], mom_v[b, rows], rot_r[owner, rows].astype(F32)
+            )
+
+    loop(NBD, keep)
+    wait_bytes(upd_r.at[pl.ds(0, NF - 1)], upd_rs)
+
     def take(b):
-        strips[b] = rot_r[owner_s[b]]
+        out_u[b] = upd_r[owner_s[b]]
 
     loop(NBD, take)
-    save = pltpu.make_async_copy(strips, rot_o, out_sem.at[0])
-    save.start()
-    wait_bytes(upd_s.at[pl.ds(0, NF - 1)], upd_rs)
 
     wait_bytes(other, core_ss)
     wait_bytes(relay_s, relay_ss)
@@ -464,45 +499,6 @@
     wait_bytes(rot_s.at[pl.ds(0, NF - 1), pl.ds(0, KEEP)], kept_ss)
     wait_bytes(dir_s.at[pl.ds(0, NF - 1)], dir_ss)
     wait_bytes(upd_s.at[pl.ds(0, NF - 1)], upd_ss)
-    save.wait()
-    save_own.wait()
-
-
-def keep_kernel(
-    owners, rot, upd, first, second, out_u, out_m, out_v,
-    mom_m, mom_v, rows_r, rows_u, new_m, new_v, in_sem, out_sem,
-):
-    base = lax.axis_index("dp") * NBD
-    copies = []
-    for b in range(NBD):
-        copies.append(
-            [
-                pltpu.make_async_copy(first.at[b], mom_m.at[b], in_sem.at[b, 0]),
-                pltpu.make_async_copy(second.at[b], mom_v.at[b], in_sem.at[b, 1]),
-                pltpu.make_async_copy(rot.at[b], rows_r.at[b], in_sem.at[b, 2]),
-                pltpu.make_async_copy(upd.at[owners[base + b]], rows_u.at[b], in_sem.at[b, 3]),
-            ]
-        )
-        for copy in copies[b]:
-            copy.start()
-    saves = []
-    for b in range(NBD):
-        for copy in copies[b]:
-            copy.wait()
-
-        def step(i, carry, b=b):
-            rows = pl.ds(pl.multiple_of(i * 16, 16), 16)
-            new_m[b, rows], new_v[b, rows] = new_moments(
-                mom_m[b, rows], mom_v[b, rows], rows_r[b, rows].astype(F32)
-            )
-            return carry
-
-        lax.fori_loop(0, ROWS // 16, step, 0)
-        for n, (source, target) in enumerate(((rows_u, out_u), (new_m, out_m), (new_v, out_v))):
-            saves.append(pltpu.make_async_copy(source.at[b], target.at[b], out_sem.at[b, n]))
-            saves[-1].start()
-    for save in saves:
-        save.wait()
 
 
 def shards(partials, first_moment, second_moment, step_counts, owners, left_basis, right_basis):
@@ -512,11 +508,11 @@
     any_space = pl.BlockSpec(memory_space=pl.ANY)
     scalars = pl.BlockSpec(memory_space=pltpu.SMEM)
     dma = pltpu.SemaphoreType.DMA
-    rotated, update = pl.pallas_call(
+    return pl.pallas_call(
         kernel,
-        out_shape=(jax.ShapeDtypeStruct(strips, BF16), jax.ShapeDtypeStruct(slots, BF16)),
+        out_shape=(pltpu.VMEM(strips, BF16), pltpu.VMEM(strips, F32), pltpu.VMEM(strips, F32)),
         in_specs=[scalars] * 2 + [any_space] * 5,
-        out_specs=(any_space,) * 2,
+        out_specs=(pl.BlockSpec(memory_space=pltpu.VMEM),) * 3,
         scratch_shapes=[
             pltpu.SMEM((NF,), jnp.int32),
             pltpu.SMEM((NBD,), jnp.int32),
@@ -535,6 +531,7 @@
             pltpu.VMEM((BS, BS), BF16),
             pltpu.VMEM((BS, BS), BF16),
             pltpu.VMEM((BS, BS), BF16),
+            pltpu.VMEM((BS, BS), F32),
             pltpu.VMEM(strips, F32),
             pltpu.VMEM(strips, F32),
             pltpu.VMEM((NF, 2, KEEP, BS), BF16),
@@ -544,7 +541,7 @@
             pltpu.VMEM((NF, BACK, BS), BF16),
             pltpu.VMEM(slots, BF16),
             pltpu.VMEM(slots, BF16),
-            pltpu.VMEM(strips, BF16),
+            pltpu.VMEM(slots, BF16),
             dma((NCH,)),
             dma((4,)),
             dma,
@@ -558,42 +555,19 @@
             dma,
             dma,
             dma,
+            dma((BACK // SLICE, NF)),
+            dma,
+            dma,
+            dma,
             dma((NF,)),
             dma,
             dma,
-            dma,
-            dma((NF,)),
-            dma,
-            dma,
-            dma((2,)),
         ],
         compiler_params=pltpu.CompilerParams(
-            collective_id=0, has_side_effects=True, vmem_limit_bytes=60 * 2**20
+            collective_id=0, has_side_effects=True, vmem_limit_bytes=52 * 2**20
         ),
         name="soap_step",
     )(owners, step_counts, part, first_moment, second_moment, left_basis[0, 0], right_basis[0, 0])
-    return pl.pallas_call(
-        keep_kernel,
-        out_shape=(
-            jax.ShapeDtypeStruct(strips, BF16),
-            jax.ShapeDtypeStruct(strips, F32),
-            jax.ShapeDtypeStruct(strips, F32),
-        ),
-        in_specs=[scalars] + [any_space] * 4,
-        out_specs=(any_space,) * 3,
-        scratch_shapes=[
-            pltpu.VMEM(strips, F32),
-            pltpu.VMEM(strips, F32),
-            pltpu.VMEM(strips, BF16),
-            pltpu.VMEM(strips, BF16),
-            pltpu.VMEM(strips, F32),
-            pltpu.VMEM(strips, F32),
-            dma((NBD, 4)),
-            dma((NBD, 3)),
-        ],
-        compiler_params=pltpu.CompilerParams(vmem_limit_bytes=60 * 2**20),
-        name="keep_moments",
-    )(owners, rotated, update, first_moment, second_moment)
 
 
 def solution(mesh):

time: 130 us -> 128 us (0.985)
  Pallas kernels: 129 us -> 123 us
  local copies, waits for them, and re-layouts: 0 us -> 3.61 us
    pallas_call x2 -> x1, Pallas kernels: 129 us -> 123 us  [shards(): pl.pallas_call(kernel, out_shape=(pltpu.VMEM(strips, BF16), pltpu.VMEM(st...]
    unnamed x0 -> x3, local copies, waits for them, and re-layouts: none -> 3.61 us
where the time goes in v3:
time: 128 us; the launch traced here: 127 us
  Pallas kernels  123 us (96%)
  local copies, waits for them, and re-layouts  3.61 us (3%)
    pallas_call x1, Pallas kernels, shards(): pl.pallas_call(kernel, out_shape=(pltpu.VMEM(strips, BF16), pltpu.VMEM(st...  123 us
    unnamed x3, local copies, waits for them, and re-layouts  3.61 us

profile of v3, /device:TPU:0, one launch (start us, length us, event | category | flops | bytes accessed | tf_op | source)
XLA Modules:
  0.0 127.1 jit_solution(18363498915371411080)
XLA Ops:
  0.6 122.8 %soap_step.1 = (bf16[8,64,1024]{2,1,0:T(8,128)(2,1)S(1)}, f32[8,64,1024]{2,1,0:T(8,128)S(1)}, f32[8,64,1024]{2,1,0:T(8,128)S(1)}) custom-call(s32[64]{0:T(128)} %owners.1, s32[64]{0:T(128)} %counts.1, bf16[4,2,8,64,1024]{4,3,2,1,0:T(8,128)(2,1)} %bitcast.3, f32[8,64,1024]{2,1,0:T(8,128)} %first.1, f32[8,64,1024]{2,1,0:T(8,128)} %second.1, ...), custom_call_target="tpu_custom_call" | custom-call | tf_op jit(solution)/shard_map/soap_step/pallas_call | solution.py:511
  123.5 1.0 copy.13
  124.5 1.3 %copy.14 = f32[8,64,1024]{2,1,0:T(8,128)} copy(f32[8,64,1024]{2,1,0:T(8,128)S(1)} %get-tuple-element.4) | data formatting | bytes 4194304
  125.8 1.3 %copy.15 = f32[8,64,1024]{2,1,0:T(8,128)} copy(f32[8,64,1024]{2,1,0:T(8,128)S(1)} %get-tuple-element.5) | data formatting | bytes 4194304

commit v4 on v3

--- a/solution.py
+++ b/solution.py
@@ -24,12 +24,14 @@
 GROUP = SIDE * ROWS
 NCH = 8
 CW = BS // NCH
+RELAY_LAG = 2
+GRAD_LAG = 4
 PAIR = 2
 FIRST = BS - PAIR * CW
 KEEP = 16
 BACK = ROWS - KEEP
 SLICE = 16
-PIECE = ROWS // 2
+PIECE = ROWS // 4
 TURNS = (2, 1, 3, 0)
 PARTS = (
     ((2, 2), (2, 1), (2, 3)),
@@ -311,19 +313,19 @@
             send_ahead()
             turn_basis()
 
-        @pl.when((t >= 1) & (t < NCH + 1))
+        @pl.when((t >= RELAY_LAG) & (t < NCH + RELAY_LAG))
         def _():
-            sum_relayed(t - 1)
-
-        @pl.when(t >= 2)
+            sum_relayed(t - RELAY_LAG)
+
+        @pl.when(t >= GRAD_LAG)
         def _():
-            send_grad(t - 2)
+            send_grad(t - GRAD_LAG)
 
     send_core(0)
     send_core(1)
     for copy in in_copies:
         copy.start()
-    loop(NCH + 2, chunk)
+    loop(NCH + GRAD_LAG, chunk)
     loop(NCH // PAIR - 1, turn_left)
 
     def begin(q):
@@ -469,7 +471,8 @@
         send_part(n, lambda j: send_update(j, 0))
 
     loop(SIDE, back_left)
-    loop(NF - 1, lambda n: send_update(to_nth(n), PIECE))
+    for at in range(PIECE, ROWS, PIECE):
+        loop(NF - 1, lambda n, at=at: send_update(to_nth(n), at))
     upd_r[me] = upd_s[me]
 
     wait_bytes(rot_r.at[pl.ds(0, NF - 1), pl.ds(0, KEEP)], kept_rs)

time: 128 us -> 125 us (0.977)
  Pallas kernels: 123 us -> 120 us
    pallas_call x1, Pallas kernels: 123 us -> 120 us  [shards(): pl.pallas_call(kernel, out_shape=(pltpu.VMEM(strips, BF16), pltpu.VMEM(st...]
where the time goes in v4:
time: 125 us
  Pallas kernels  120 us (96%)
  local copies, waits for them, and re-layouts  3.61 us (3%)
    pallas_call x1, Pallas kernels, shards(): pl.pallas_call(kernel, out_shape=(pltpu.VMEM(strips, BF16), pltpu.VMEM(st...  120 us
    unnamed x3, local copies, waits for them, and re-layouts  3.61 us

profile of v4, /device:TPU:0, one launch (start us, length us, event | category | flops | bytes accessed | tf_op | source)
XLA Modules:
  0.0 124.6 jit_solution(16315500147898399188)
XLA Ops:
  0.6 120.3 %soap_step.1 = (bf16[8,64,1024]{2,1,0:T(8,128)(2,1)S(1)}, f32[8,64,1024]{2,1,0:T(8,128)S(1)}, f32[8,64,1024]{2,1,0:T(8,128)S(1)}) custom-call(s32[64]{0:T(128)} %owners.1, s32[64]{0:T(128)} %counts.1, bf16[4,2,8,64,1024]{4,3,2,1,0:T(8,128)(2,1)} %bitcast.3, f32[8,64,1024]{2,1,0:T(8,128)} %first.1, f32[8,64,1024]{2,1,0:T(8,128)} %second.1, ...), custom_call_target="tpu_custom_call" | custom-call | tf_op jit(solution)/shard_map/soap_step/pallas_call | solution.py:514
  121.0 1.0 copy.13
  121.9 1.3 %copy.14 = f32[8,64,1024]{2,1,0:T(8,128)} copy(f32[8,64,1024]{2,1,0:T(8,128)S(1)} %get-tuple-element.4) | data formatting | bytes 4194304
  123.3 1.3 %copy.15 = f32[8,64,1024]{2,1,0:T(8,128)} copy(f32[8,64,1024]{2,1,0:T(8,128)S(1)} %get-tuple-element.5) | data formatting | bytes 4194304

commit v5 on v4

--- a/solution.py
+++ b/solution.py
@@ -436,19 +436,19 @@
             preferred_element_type=F32,
         ).astype(BF16)
 
-    loop(SIDE - 1, back_right)
+    loop(SIDE // 2, back_right)
 
     def begin_left(q):
         rows = pl.ds(pl.multiple_of(q * GROUP, GROUP), GROUP)
         total = None
-        for n in range(SIDE - 1):
+        for n in range(SIDE // 2):
             _, used = turn_rows(n)
             part_n = jnp.dot(lmat[rows, used], half[used, :], preferred_element_type=F32)
             total = part_n if total is None else total + part_n
         begun[rows, :] = total
 
     loop(SIDE, begin_left)
-    back_right(SIDE - 1)
+    loop(SIDE // 2, lambda n: back_right(n + SIDE // 2))
 
     def send_update(j, at):
         pltpu.make_async_remote_copy(
@@ -462,10 +462,12 @@
 
     def back_left(n):
         yy, rows = turn_rows(n)
-        _, last = turn_rows(SIDE - 1)
+        total = begun[rows, :]
+        for m in range(SIDE // 2, SIDE):
+            _, used = turn_rows(m)
+            total += jnp.dot(lmat[rows, used], half[used, :], preferred_element_type=F32)
         upd_s[pl.ds(yy * SIDE, SIDE)] = (
-            (begun[rows, :] + jnp.dot(lmat[rows, last], half[last, :], preferred_element_type=F32))
-            .astype(BF16)
+            total.astype(BF16)
             .reshape(SIDE, ROWS, BS)
         )
         send_part(n, lambda j: send_update(j, 0))

time: 125 us -> 124 us (level)
  no operation moved by 1% of the time
where the time goes in v5:
time: 124 us
  Pallas kernels  120 us (97%)
  local copies, waits for them, and re-layouts  3.61 us (3%)
    pallas_call x1, Pallas kernels, shards(): pl.pallas_call(kernel, out_shape=(pltpu.VMEM(strips, BF16), pltpu.VMEM(st...  120 us
    unnamed x3, local copies, waits for them, and re-layouts  3.61 us

profile of v5, /device:TPU:0, one launch (start us, length us, event | category | flops | bytes accessed | tf_op | source)
XLA Modules:
  0.0 123.9 jit_solution(9622056405403483974)
XLA Ops:
  0.6 119.7 %soap_step.1 = (bf16[8,64,1024]{2,1,0:T(8,128)(2,1)S(1)}, f32[8,64,1024]{2,1,0:T(8,128)S(1)}, f32[8,64,1024]{2,1,0:T(8,128)S(1)}) custom-call(s32[64]{0:T(128)} %owners.1, s32[64]{0:T(128)} %counts.1, bf16[4,2,8,64,1024]{4,3,2,1,0:T(8,128)(2,1)} %bitcast.3, f32[8,64,1024]{2,1,0:T(8,128)} %first.1, f32[8,64,1024]{2,1,0:T(8,128)} %second.1, ...), custom_call_target="tpu_custom_call" | custom-call | tf_op jit(solution)/shard_map/soap_step/pallas_call | solution.py:516
  120.3 1.0 copy.13
  121.3 1.3 %copy.14 = f32[8,64,1024]{2,1,0:T(8,128)} copy(f32[8,64,1024]{2,1,0:T(8,128)S(1)} %get-tuple-element.4) | data formatting | bytes 4194304
  122.6 1.3 %copy.15 = f32[8,64,1024]{2,1,0:T(8,128)} copy(f32[8,64,1024]{2,1,0:T(8,128)S(1)} %get-tuple-element.5) | data formatting | bytes 4194304
